TPU v7x, 32 devices: a whole 2x2x4 slice. The times are simulated.
32 devices in a mesh: grp: 2 (over y), seq: 16 (over z, x, core).
Axes of the slice: x: 2, y: 2, z: 4, core: 2. Of those that a mesh axis runs over, the one named last changes fastest.
Arguments:
- query_rows: bfloat16 [6144, 4096], P(('grp', 'seq')), parts along dimension 0, may hold values from -0.59765625 to 0.59765625
- key_rows: bfloat16 [6144, 4096], P(('grp', 'seq')), parts along dimension 0, may hold values from -0.59765625 to 0.59765625
- value_rows: bfloat16 [6144, 4096], P(('grp', 'seq')), parts along dimension 0, may hold values from -0.59765625 to 0.59765625
- log_decay: float32 [32, 6144], P(None, ('grp', 'seq')), parts along dimension 1, may hold values from -1 to 0, as said below
- out_grad: bfloat16 [6144, 4096], P(('grp', 'seq')), parts along dimension 0, may hold values from -0.59765625 to 0.59765625
Outputs:
- attended: bfloat16 [6144, 4096], P(('grp', 'seq')), parts along dimension 0
- query_grad: bfloat16 [6144, 4096], P(('grp', 'seq')), parts along dimension 0
- key_grad: bfloat16 [6144, 4096], P(('grp', 'seq')), parts along dimension 0
- value_grad: bfloat16 [6144, 4096], P(('grp', 'seq')), parts along dimension 0
There are 2 independent parts, one for each index of `grp`. A program takes and returns all parts, laid end to end along the dimension named above; each array names one. Nothing has to cross between parts.
Inputs may be any that keep to these rules, and one draw needn't show every extreme that they name: `log_decay`: strictly negative.
All inputs are finite; a program needn't handle non-finite values.
Results may differ from a plain program's by a relative error of at most 0.0057.
Values sent between devices are 32-bit elements; how exact they have to be, the bound alone decides.
A program may use at most 128 MiB of HBM per device.

v0:
```python
import jax
import jax.numpy as jnp
from jax import lax
from jax.sharding import PartitionSpec as P


def partner_2(value, axis, bit):
    mask = 2**bit
    pairs = [(source, source ^ mask) for source in range(lax.axis_size(axis))]
    return lax.ppermute(value, axis, pairs)


def decay_terms(log_decay):
    cumulative = jnp.cumsum(log_decay, axis=1)
    block_total = cumulative[:, -1:]
    length = log_decay.shape[1]
    row_index = lax.broadcasted_iota(jnp.int32, (length, length), 0)
    col_index = lax.broadcasted_iota(jnp.int32, (length, length), 1)
    causal = (col_index <= row_index)[None]
    log_gaps = cumulative[:, :, None] - cumulative[:, None, :]
    decay_mask = jnp.where(causal, jnp.exp(jnp.where(causal, log_gaps, 0.0)), 0.0)
    return (cumulative, block_total, decay_mask)


def combine_states(earlier, later):
    return (earlier[0] * later[0], later[0][:, None, None] * earlier[1] + later[1])


def choose_tree(flag, first, second):
    return jax.tree.map(
        lambda first_leaf, second_leaf: jnp.where(flag, first_leaf, second_leaf), first, second
    )


def hypercube_states(forward_own, backward_own, identity):
    levels = lax.axis_size("seq").bit_length() - 1
    element_offset = lax.axis_index("seq")
    forward_total, backward_total = (forward_own, backward_own)
    forward_before, backward_after = (identity, identity)
    for bit_number in range(levels):
        partner = partner_2(
            (forward_total[0], forward_total[1], backward_total[0], backward_total[1]),
            "seq",
            bit_number,
        )
        partner_forward = (partner[0], partner[1])
        partner_backward = (partner[2], partner[3])
        is_upper = element_offset // 2**bit_number % 2 == 1
        forward_before = choose_tree(
            is_upper, combine_states(partner_forward, forward_before), forward_before
        )
        forward_total = choose_tree(
            is_upper,
            combine_states(partner_forward, forward_total),
            combine_states(forward_total, partner_forward),
        )
        backward_after = choose_tree(
            is_upper, backward_after, combine_states(partner_backward, backward_after)
        )
        backward_total = choose_tree(
            is_upper,
            combine_states(backward_total, partner_backward),
            combine_states(partner_backward, backward_total),
        )
    return (forward_before[1], backward_after[1])


def on_device(query_rows, key_rows, value_rows, log_decay, out_grad):
    heads = log_decay.shape[0]
    length = log_decay.shape[1]
    width = query_rows.shape[1] // heads
    queries = query_rows.reshape(length, heads, width)
    keys_local = key_rows.reshape(length, heads, width)
    values = value_rows.reshape(length, heads, width)
    grads_out = out_grad.reshape(length, heads, width)
    cumulative, block_total, decay_mask = decay_terms(log_decay)
    to_query = jnp.exp(cumulative).T[:, :, None]
    to_end = jnp.exp(block_total - cumulative).T[:, :, None]
    carried = jnp.exp(block_total[:, 0])
    weighted_keys = (keys_local.astype(jnp.float32) * to_end).astype(jnp.bfloat16)
    local_state = jnp.einsum(
        "thd,the->hde", weighted_keys, values, preferred_element_type=jnp.float32
    )
    scaled_queries = (queries.astype(jnp.float32) * to_query).astype(jnp.bfloat16)
    local_grad = jnp.einsum(
        "thd,the->hde", scaled_queries, grads_out, preferred_element_type=jnp.float32
    )
    identity = (jnp.ones((heads,), jnp.float32), jnp.zeros((heads, width, width), jnp.float32))
    state_in, state_after = hypercube_states(
        (carried, local_state), (carried, local_grad), identity
    )
    scores = jnp.einsum("thd,shd->hts", queries, keys_local, preferred_element_type=jnp.float32)
    attn_weights = (scores * decay_mask).astype(jnp.bfloat16)
    grad_scores = (
        jnp.einsum("the,she->hts", grads_out, values, preferred_element_type=jnp.float32)
        * decay_mask
    ).astype(jnp.bfloat16)
    state_in_rounded = state_in.astype(jnp.bfloat16)
    grad_rounded = state_after.astype(jnp.bfloat16)
    attended = jnp.einsum("hts,she->the", attn_weights, values, preferred_element_type=jnp.float32)
    attended = attended + to_query * jnp.einsum(
        "thd,hde->the", queries, state_in_rounded, preferred_element_type=jnp.float32
    )
    query_grad = jnp.einsum(
        "hts,shd->thd", grad_scores, keys_local, preferred_element_type=jnp.float32
    )
    query_grad = query_grad + to_query * jnp.einsum(
        "the,hde->thd", grads_out, state_in_rounded, preferred_element_type=jnp.float32
    )
    key_grad = jnp.einsum("hts,thd->shd", grad_scores, queries, preferred_element_type=jnp.float32)
    key_grad = key_grad + to_end * jnp.einsum(
        "she,hde->shd", values, grad_rounded, preferred_element_type=jnp.float32
    )
    value_grad = jnp.einsum(
        "hts,the->she", attn_weights, grads_out, preferred_element_type=jnp.float32
    )
    value_grad = value_grad + to_end * jnp.einsum(
        "shd,hde->she", keys_local, grad_rounded, preferred_element_type=jnp.float32
    )

    def join_rows(array):
        return array.astype(jnp.bfloat16).reshape(length, heads * width)

    return (join_rows(attended), join_rows(query_grad), join_rows(key_grad), join_rows(value_grad))


def solution(mesh):
    in_specs = (
        P(("grp", "seq"), None),
        P(("grp", "seq"), None),
        P(("grp", "seq"), None),
        P(None, ("grp", "seq")),
        P(("grp", "seq"), None),
    )
    out_specs = (
        P(("grp", "seq"), None),
        P(("grp", "seq"), None),
        P(("grp", "seq"), None),
        P(("grp", "seq"), None),
    )
    return jax.shard_map(
        on_device, mesh=mesh, in_specs=in_specs, out_specs=out_specs, check_vma=False
    )
```

profile of v0, /device:TPU:0, one launch (start us, length us, event | category | flops | bytes accessed | tf_op | source)
XLA Modules:
  0.0 417.8 jit_solution(7170468877316356271)
XLA Ops:
  0.6 0.0 copy-start
  0.6 0.9 copy_bitcast_fusion.5
  1.5 0.6 reduce-window.6
  2.1 0.2 slice_reduce_fusion
  2.3 0.1 copy_bitcast_fusion.4
  2.4 0.2 slice_reduce_fusion.1
  2.6 0.1 fusion.62
  2.7 0.0 copy-start.2
  2.7 0.0 copy-start.5
  2.7 5.0 %fusion.10 = f32[32,128,128]{2,1,0:T(8,128)} fusion(f32[192,32]{0,1:T(8,128)S(1)} %get-tuple-element.12, bf16[192,4096]{1,0:T(8,128)(2,1)S(1)} %copy-done, bf16[192,4096]{1,0:T(8,128)(2,1)} %param.6), kind=kOutput, calls=%fused_computation.31 | convolution fusion | flops 203685888 | bytes 5267456 | tf_op jit(solution)/shard_map/thd,the->hde/dot_general | solution.py:81
  7.7 0.5 collective-permute-start.3
  8.1 3.3 fusion.11
  11.4 0.1 collective-permute-start.7
  11.5 0.5 collective-permute-start
  11.9 3.3 collective-permute-done
  15.2 0.7 collective-permute-done.7
  15.9 6.9 %add_select_fusion.8 = (f32[32,128,128]{2,1,0:T(8,128)}, f32[32,128,128]{2,1,0:T(8,128)}) fusion(f32[32,128,128]{2,1,0:T(8,128)} %fusion.11, f32[32,128,128]{2,1,0:T(8,128)} %collective-permute-done.7, f32[32]{0:T(128)S(1)} %collective-permute-done, f32[32]{0:T(128)S(1)} %exp.18, pred[]{:T(512)S(6)} %eq.20, f32[32,128,128]{2,1,0:T(8,128)} %collective-permute-done.3, ...), kind=kLoop, calls=%fused_computation.27 | loop fusion | flops 5242880 | bytes 12583169 | tf_op jit(solution)/shard_map/jit(_where)/select_n | solution.py:31
  22.8 2.7 collective-permute-start.8
  25.5 0.0 collective-permute-start.4
  25.5 2.0 collective-permute-start.1
  27.5 89.4 %collective-permute-done.1 = f32[32]{0:T(128)S(1)} collective-permute-done((f32[32]{0:T(128)S(1)}, f32[32]{0:T(128)S(1)}, u32[]{:S(2)}, u32[]{:S(2)}) %collective-permute-start.1) | collective-permute-done | bytes 160 | tf_op jit(solution)/shard_map/ppermute | solution.py:10
  116.9 7.0 %add_select_fusion.7 = (f32[32,128,128]{2,1,0:T(8,128)}, f32[32,128,128]{2,1,0:T(8,128)}) fusion(f32[32,128,128]{2,1,0:T(8,128)} %get-tuple-element.20, f32[32,128,128]{2,1,0:T(8,128)} %collective-permute-done.8, f32[32]{0:T(128)S(1)} %collective-permute-done.1, f32[32]{0:T(128)S(1)} %exponential_multiply_fusion, pred[]{:T(512)S(6)} %eq.19, ...), kind=kLoop, calls=%fused_computation.26 | loop fusion | flops 5242880 | bytes 12583169 | tf_op jit(solution)/shard_map/jit(_where)/select_n | solution.py:31
  123.9 1.8 collective-permute-start.9
  125.7 0.2 collective-permute-start.5
  125.9 3.1 multiply_convert_fusion
  129.0 1.8 collective-permute-start.2
  130.8 85.6 %collective-permute-done.2 = f32[32]{0:T(128)S(1)} collective-permute-done((f32[32]{0:T(128)S(1)}, f32[32]{0:T(128)S(1)}, u32[]{:S(2)}, u32[]{:S(2)}) %collective-permute-start.2) | collective-permute-done | bytes 160 | tf_op jit(solution)/shard_map/ppermute | solution.py:10
  216.5 7.1 %add_select_fusion.6 = (f32[32,128,128]{2,1,0:T(8,128)}, f32[32,128,128]{2,1,0:T(8,128)}) fusion(f32[32,128,128]{2,1,0:T(8,128)} %get-tuple-element.18, f32[32,128,128]{2,1,0:T(8,128)} %collective-permute-done.9, f32[32]{0:T(128)S(1)} %collective-permute-done.2, f32[32]{0:T(128)S(1)} %mul.95, pred[]{:T(512)S(6)} %eq.18, ...), kind=kLoop, calls=%fused_computation.25 | loop fusion | flops 5242880 | bytes 12583169 | tf_op jit(solution)/shard_map/jit(_where)/select_n | solution.py:31
  223.6 2.6 collective-permute-start.10
  226.2 3.0 fusion.28
  229.2 2.6 fusion.23
  231.9 2.4 multiply_convert_fusion.1
  234.3 0.4 collective-permute-start.6
  234.7 1.3 copy-done.11
  236.0 3.0 fusion.12
  239.0 2.9 fusion.20
  241.9 120.2 %collective-permute-done.10 = f32[32,128,128]{2,1,0:T(8,128)} collective-permute-done((f32[32,128,128]{2,1,0:T(8,128)}, f32[32,128,128]{2,1,0:T(8,128)}, u32[]{:S(2)}, u32[]{:S(2)}) %collective-permute-start.10) | collective-permute-done | bytes 2097184 | tf_op jit(solution)/shard_map/ppermute | solution.py:10
  362.1 4.5 %fusion.9 = bf16[32,128,128]{2,1,0:T(8,128)(2,1)S(1)} fusion(f32[32,128,128]{2,1,0:T(8,128)} %collective-permute-done.10, f32[32,128,128]{2,1,0:T(8,128)} %collective-permute-done.9, f32[32,128,128]{2,1,0:T(8,128)} %collective-permute-done.8, f32[32,128,128]{2,1,0:T(8,128)} %collective-permute-done.7, f32[32]{0:T(128)S(1)} %get-tuple-element.4, ...), kind=kLoop, calls=%fused_computation.24 | loop fusion | flops 5767168 | bytes 9437572 | tf_op jit(solution)/shard_map/convert_element_type | solution.py:99
  366.6 1.2 fusion.40
  367.8 0.7 copy-done.10
  368.5 1.1 fusion.43
  369.6 36.5 %collective-permute-done.6 = f32[32,128,128]{2,1,0:T(8,128)} collective-permute-done((f32[32,128,128]{2,1,0:T(8,128)}, f32[32,128,128]{2,1,0:T(8,128)}, u32[]{:S(2)}, u32[]{:S(2)}) %collective-permute-start.6) | collective-permute-done | bytes 2097184 | tf_op jit(solution)/shard_map/ppermute | solution.py:10
  406.1 4.9 %fusion.8 = bf16[32,128,128]{2,1,0:T(8,128)(2,1)S(1)} fusion(f32[32,128,128]{2,1,0:T(8,128)} %collective-permute-done.3, f32[32,128,128]{2,1,0:T(8,128)} %collective-permute-done.4, f32[32,128,128]{2,1,0:T(8,128)} %collective-permute-done.5, f32[32,128,128]{2,1,0:T(8,128)} %collective-permute-done.6, f32[32]{0:T(128)S(1)} %get-tuple-element.15, ...), kind=kLoop, calls=%fused_computation.23 | loop fusion | flops 5767168 | bytes 9437572 | tf_op jit(solution)/shard_map/convert_element_type | solution.py:98
  411.0 1.2 fusion.37
  412.2 0.2 copy-done.7
  412.4 1.1 fusion.34
  413.5 2.2 copy_bitcast_fusion.2
  415.6 2.1 copy_bitcast_fusion
  (32 shorter events, 0.1 us)
Async XLA Ops:
  0.6 2.0 copy-start
  2.7 5.4 %copy-start.2 = (bf16[192,4096]{1,0:T(8,128)(2,1)S(1)}, bf16[192,4096]{1,0:T(8,128)(2,1)}, u32[]{:S(2)}) copy-start(bf16[192,4096]{1,0:T(8,128)(2,1)} %param.9) | copy-start | bytes 4718596
  2.7 5.4 %copy-start.5 = (bf16[192,4096]{1,0:T(8,128)(2,1)S(1)}, bf16[192,4096]{1,0:T(8,128)(2,1)}, u32[]{:S(2)}) copy-start(bf16[192,4096]{1,0:T(8,128)(2,1)} %param.5) | copy-start | bytes 4718596
  7.7 7.6 %collective-permute-start.3 = (f32[32,128,128]{2,1,0:T(8,128)}, f32[32,128,128]{2,1,0:T(8,128)}, u32[]{:S(2)}, u32[]{:S(2)}) collective-permute-start(f32[32,128,128]{2,1,0:T(8,128)} %fusion.10), channel_id=1, source_target_pairs={{0,1},{1,0},{2,3},{3,2},{4,5},{5,4},{6,7},{7,6},{8,9},{9,8},{10,11... | collective-permute-start | bytes 6291464 | tf_op jit(solution)/shard_map/ppermute | solution.py:10
  11.4 4.5 %collective-permute-start.7 = (f32[32,128,128]{2,1,0:T(8,128)}, f32[32,128,128]{2,1,0:T(8,128)}, u32[]{:S(2)}, u32[]{:S(2)}) collective-permute-start(f32[32,128,128]{2,1,0:T(8,128)} %fusion.11), channel_id=1, source_target_pairs={{0,1},{1,0},{2,3},{3,2},{4,5},{5,4},{6,7},{7,6},{8,9},{9,8},{10,11... | collective-permute-start | bytes 6291464 | tf_op jit(solution)/shard_map/ppermute | solution.py:10
  11.5 3.8 collective-permute-start
  22.8 94.1 %collective-permute-start.8 = (f32[32,128,128]{2,1,0:T(8,128)}, f32[32,128,128]{2,1,0:T(8,128)}, u32[]{:S(2)}, u32[]{:S(2)}) collective-permute-start(f32[32,128,128]{2,1,0:T(8,128)} %get-tuple-element.20), channel_id=1, source_target_pairs={{0,2},{1,3},{2,0},{3,1},{4,6},{5,7},{6,4},{7,5},{8,10},{9,11},{10,... | collective-permute-start | bytes 6291464 | tf_op jit(solution)/shard_map/ppermute | solution.py:10
  25.5 91.4 %collective-permute-start.4 = (f32[32,128,128]{2,1,0:T(8,128)}, f32[32,128,128]{2,1,0:T(8,128)}, u32[]{:S(2)}, u32[]{:S(2)}) collective-permute-start(f32[32,128,128]{2,1,0:T(8,128)} %get-tuple-element.21), channel_id=1, source_target_pairs={{0,2},{1,3},{2,0},{3,1},{4,6},{5,7},{6,4},{7,5},{8,10},{9,11},{10,... | collective-permute-start | bytes 6291464 | tf_op jit(solution)/shard_map/ppermute | solution.py:10
  25.5 91.4 %collective-permute-start.1 = (f32[32]{0:T(128)S(1)}, f32[32]{0:T(128)S(1)}, u32[]{:S(2)}, u32[]{:S(2)}) collective-permute-start(f32[32]{0:T(128)S(1)} %exponential_multiply_fusion), channel_id=1, source_target_pairs={{0,2},{1,3},{2,0},{3,1},{4,6},{5,7},{6,4},{7,5},{8,10},{9,11},{10,... | collective-permute-start | bytes 392 | tf_op jit(solution)/shard_map/ppermute | solution.py:10
  123.9 92.6 %collective-permute-start.9 = (f32[32,128,128]{2,1,0:T(8,128)}, f32[32,128,128]{2,1,0:T(8,128)}, u32[]{:S(2)}, u32[]{:S(2)}) collective-permute-start(f32[32,128,128]{2,1,0:T(8,128)} %get-tuple-element.18), channel_id=1, source_target_pairs={{0,4},{1,5},{2,6},{3,7},{4,0},{5,1},{6,2},{7,3},{8,12},{9,13},{10,... | collective-permute-start | bytes 6291464 | tf_op jit(solution)/shard_map/ppermute | solution.py:10
  125.7 90.8 %collective-permute-start.5 = (f32[32,128,128]{2,1,0:T(8,128)}, f32[32,128,128]{2,1,0:T(8,128)}, u32[]{:S(2)}, u32[]{:S(2)}) collective-permute-start(f32[32,128,128]{2,1,0:T(8,128)} %get-tuple-element.19), channel_id=1, source_target_pairs={{0,4},{1,5},{2,6},{3,7},{4,0},{5,1},{6,2},{7,3},{8,12},{9,13},{10,... | collective-permute-start | bytes 6291464 | tf_op jit(solution)/shard_map/ppermute | solution.py:10
  129.0 87.4 %collective-permute-start.2 = (f32[32]{0:T(128)S(1)}, f32[32]{0:T(128)S(1)}, u32[]{:S(2)}, u32[]{:S(2)}) collective-permute-start(f32[32]{0:T(128)S(1)} %mul.95), channel_id=1, source_target_pairs={{0,4},{1,5},{2,6},{3,7},{4,0},{5,1},{6,2},{7,3},{8,12},{9,13},{10,... | collective-permute-start | bytes 392 | tf_op jit(solution)/shard_map/ppermute | solution.py:10
  130.8 95.4 %copy-start.6 = (bf16[192,4096]{1,0:T(8,128)(2,1)S(1)}, bf16[192,4096]{1,0:T(8,128)(2,1)}, u32[]{:S(2)}) copy-start(bf16[192,4096]{1,0:T(8,128)(2,1)} %param.5) | copy-start | bytes 4718596
  216.5 9.7 %copy-start.12 = (bf16[32,192,192]{2,1,0:T(8,128)(2,1)S(1)}, bf16[32,192,192]{2,1,0:T(8,128)(2,1)}, u32[]{:S(2)}) copy-start(bf16[32,192,192]{2,1,0:T(8,128)(2,1)} %multiply_convert_fusion) | copy-start | bytes 7077892
  223.6 5.6 %copy-start.1 = (bf16[192,4096]{1,0:T(8,128)(2,1)S(1)}, bf16[192,4096]{1,0:T(8,128)(2,1)}, u32[]{:S(2)}) copy-start(bf16[192,4096]{1,0:T(8,128)(2,1)} %param.6) | copy-start | bytes 4718596
  223.6 138.5 %collective-permute-start.10 = (f32[32,128,128]{2,1,0:T(8,128)}, f32[32,128,128]{2,1,0:T(8,128)}, u32[]{:S(2)}, u32[]{:S(2)}) collective-permute-start(f32[32,128,128]{2,1,0:T(8,128)} %get-tuple-element.16), channel_id=1, source_target_pairs={{0,8},{1,9},{2,10},{3,11},{4,12},{5,13},{6,14},{7,15},{8,0},{9,1},... | collective-permute-start | bytes 6291464 | tf_op jit(solution)/shard_map/ppermute | solution.py:10
  231.9 4.1 copy-start.3
  234.3 1.7 copy-start.11
  234.3 171.8 %collective-permute-start.6 = (f32[32,128,128]{2,1,0:T(8,128)}, f32[32,128,128]{2,1,0:T(8,128)}, u32[]{:S(2)}, u32[]{:S(2)}) collective-permute-start(f32[32,128,128]{2,1,0:T(8,128)} %get-tuple-element.17), channel_id=1, source_target_pairs={{0,8},{1,9},{2,10},{3,11},{4,12},{5,13},{6,14},{7,15},{8,0},{9,1},... | collective-permute-start | bytes 6291464 | tf_op jit(solution)/shard_map/ppermute | solution.py:10
  362.1 4.5 %copy-start.9 = (f32[32,192,128]{2,1,0:T(8,128)S(1)}, f32[32,192,128]{2,1,0:T(8,128)}, u32[]{:S(2)}) copy-start(f32[32,192,128]{2,1,0:T(8,128)} %fusion.28) | copy-start | bytes 9437188
  366.6 1.9 copy-start.10
  406.1 4.9 %copy-start.4 = (bf16[192,4096]{1,0:T(8,128)(2,1)S(1)}, bf16[192,4096]{1,0:T(8,128)(2,1)}, u32[]{:S(2)}) copy-start(bf16[192,4096]{1,0:T(8,128)(2,1)} %param.9) | copy-start | bytes 4718596
  406.1 4.9 %copy-start.8 = (f32[32,192,128]{2,1,0:T(8,128)S(1)}, f32[32,192,128]{2,1,0:T(8,128)}, u32[]{:S(2)}) copy-start(f32[32,192,128]{2,1,0:T(8,128)} %fusion.23) | copy-start | bytes 9437188
  411.0 1.4 copy-start.7
where the time goes:
time: 418 us
  waiting for transfers between devices  336 us (80%)
  other arithmetic  31.3 us (7%)
  matrix products  29.8 us (7%)
  starting transfers between devices  12.5 us (3%)
  local copies, waits for them, and re-layouts  7.76 us (2%)
    ppermute x11, waiting for transfers between devices, partner_2(): return lax.ppermute(value, axis, pairs)  336 us
    select_n x4, other arithmetic, choose_tree(): jnp.where(flag, first_leaf, second_leaf)  21.1 us
    ppermute x11, starting transfers between devices, partner_2(): return lax.ppermute(value, axis, pairs)  12.5 us
  transfers between devices with their start and end apart: 11, of which 6 were waited for; matrix products, arithmetic and copies ran while one was open for 7% of the time, Pallas kernels for 0%

commit v1 on v0

v1 whole, which is shorter than its diff:
```python
import functools

import jax
import jax.numpy as jnp
from jax import lax
from jax.experimental import pallas as pl
from jax.experimental.pallas import tpu as pltpu
from jax.sharding import PartitionSpec as P

F32 = jnp.float32
BF16 = jnp.bfloat16


def dot(a, b, a_dim, b_dim):
    return lax.dot_general(a, b, (((a_dim,), (b_dim,)), ((), ())), preferred_element_type=F32)


def kernel(
    planes,
    q_ref,
    k_ref,
    v_ref,
    g_ref,
    cum_ref,
    a_ref,
    att_ref,
    qg_ref,
    kg_ref,
    vg_ref,
    pair,
    give,
    chips,
    ztx,
    zrx,
    res,
    srx,
    dec,
    dec_send,
    dec_recv,
    pair_send,
    pair_recv,
    x_send,
    x_recv,
    z_send,
    z_recv,
    s_send,
    s_recv,
):
    n = pair.shape[1]
    width = pair.shape[-1]
    length = q_ref.shape[0]
    seq = lax.axis_index("seq")
    core = lax.rem(seq, 2)
    x = lax.rem(seq // 2, 2)
    z = seq // 4
    place = 2 * x + core
    base = 4 * z
    sibling = base + 2 * x + (1 - core)
    across = base + 2 * (1 - x) + core
    diagonal = base + 2 * (1 - x) + (1 - core)
    has_down = z > 0
    has_up = z < planes - 1

    barrier = pltpu.get_barrier_semaphore()
    for peer in (sibling, across, diagonal):
        pl.semaphore_signal(barrier, inc=1, device_id={"seq": peer})

    @pl.when(has_down)
    def _():
        pl.semaphore_signal(barrier, inc=1, device_id={"seq": seq - 4})

    @pl.when(has_up)
    def _():
        pl.semaphore_signal(barrier, inc=1, device_id={"seq": seq + 4})

    pl.semaphore_wait(barrier, 3 + has_down.astype(jnp.int32) + has_up.astype(jnp.int32))

    def remote(src, dst, send, recv, peer):
        return pltpu.make_async_remote_copy(
            src_ref=src, dst_ref=dst, send_sem=send, recv_sem=recv, device_id={"seq": peer}
        )

    def dec_copy(slot, peer):
        return remote(a_ref, dec.at[place], dec_send.at[slot], dec_recv.at[slot], peer)

    def pair_copy(j):
        return remote(give.at[j], pair.at[core, j], pair_send.at[j], pair_recv.at[j], sibling)

    def x_copy(d, j):
        return remote(
            chips.at[x, d, j], chips.at[x, d, j], x_send.at[d, j], x_recv.at[d, j], across
        )

    def z_copy(d, j):
        peer = seq + 4 if d == 0 else seq - 4
        return remote(ztx.at[d, j], zrx.at[d, j], z_send.at[d, j], z_recv.at[d, j], peer)

    def s_copy(d, j):
        return remote(
            res.at[1 - core, d, j], srx.at[d, j], s_send.at[d, j], s_recv.at[d, j], sibling
        )

    dec_copies = [dec_copy(0, sibling), dec_copy(1, across), dec_copy(2, diagonal)]
    for copy in dec_copies:
        copy.start()
    dec[place] = a_ref[...]

    row_index = lax.broadcasted_iota(jnp.int32, (length, length), 0)
    col_index = lax.broadcasted_iota(jnp.int32, (length, length), 1)

    def column(row):
        return jnp.sum(jnp.where(row_index == col_index, row, 0.0), axis=1, keepdims=True)

    def lanes(head):
        return pl.ds(pl.multiple_of(head * width, width), width)

    def decay(p, head):
        return dec[p, pl.ds(head, 1), :]

    def local_states(head, dst):
        cols = lanes(head)
        row = cum_ref[pl.ds(head, 1), :]
        col = column(row)
        total = row[:, length - 1 : length]
        weighted = (k_ref[:, cols].astype(F32) * jnp.exp(total - col)).astype(BF16)
        scaled = (q_ref[:, cols].astype(F32) * jnp.exp(col)).astype(BF16)
        dst[0] = dot(weighted, v_ref[:, cols], 0, 0)
        dst[1] = dot(scaled, g_ref[:, cols], 0, 0)

    def first(i, carry):
        @pl.when(i < n)
        def _():
            local_states((1 - core) * n + i, give.at[i])
            pair_copy(i).start()
            local_states(core * n + i, pair.at[core, i])

        @pl.when(i == 1)
        def _():
            dec_copies[0].wait_recv()

        @pl.when(i >= 1)
        def _():
            j = i - 1
            head = core * n + j
            pair_copy(j).wait_recv()
            chips[x, 0, j] = decay(2 * x + 1, head) * pair[0, j, 0] + pair[1, j, 0]
            x_copy(0, j).start()
            chips[x, 1, j] = decay(2 * x, head) * pair[1, j, 1] + pair[0, j, 1]
            x_copy(1, j).start()

        return carry

    lax.fori_loop(0, n + 1, first, 0)
    dec_copies[1].wait_recv()
    dec_copies[2].wait_recv()

    @pl.when(jnp.logical_not(has_down))
    def _():
        zrx[0] = jnp.zeros(zrx.shape[1:], F32)

    @pl.when(jnp.logical_not(has_up))
    def _():
        zrx[1] = jnp.zeros(zrx.shape[1:], F32)

    def outputs(head, state, grad):
        cols = lanes(head)
        q, k, v, g = q_ref[:, cols], k_ref[:, cols], v_ref[:, cols], g_ref[:, cols]
        row = cum_ref[pl.ds(head, 1), :]
        col = column(row)
        total = row[:, length - 1 : length]
        causal = col_index <= row_index
        mask = jnp.where(causal, jnp.exp(jnp.where(causal, col - row, 0.0)), 0.0)
        weights = (dot(q, k, 1, 1) * mask).astype(BF16)
        scores = (dot(g, v, 1, 1) * mask).astype(BF16)
        to_query = jnp.exp(col)
        to_end = jnp.exp(total - col)
        state = state.astype(BF16)
        grad = grad.astype(BF16)
        att_ref[:, cols] = (dot(weights, v, 1, 0) + to_query * dot(q, state, 1, 0)).astype(BF16)
        qg_ref[:, cols] = (dot(scores, k, 1, 0) + to_query * dot(g, state, 1, 1)).astype(BF16)
        kg_ref[:, cols] = (dot(scores, q, 0, 0) + to_end * dot(v, grad, 1, 1)).astype(BF16)
        vg_ref[:, cols] = (dot(weights, g, 0, 0) + to_end * dot(k, grad, 1, 0)).astype(BF16)

    lag = jnp.maximum(z, planes - 1 - z) + 1

    def second(t, carry):
        jf = t - z

        @pl.when(jnp.logical_and(jf >= 0, jf < n))
        def _():
            head = core * n + jf
            a00, a01 = decay(0, head), decay(1, head)
            a10, a11 = decay(2, head), decay(3, head)
            x_copy(0, jf).wait_recv()

            @pl.when(has_down)
            def _():
                z_copy(0, jf).wait_recv()

            before = zrx[0, jf]
            middle = (a00 * a01) * before + chips[0, 0, jf]

            @pl.when(has_up)
            def _():
                ztx[0, jf] = (a10 * a11) * middle + chips[1, 0, jf]
                z_copy(0, jf).start()

            into = jnp.where(x == 0, before, middle)
            res[0, 0, jf] = into
            res[1, 0, jf] = decay(2 * x, head) * into + pair[0, jf, 0]
            s_copy(0, jf).start()

        jb = t - (planes - 1 - z)

        @pl.when(jnp.logical_and(jb >= 0, jb < n))
        def _():
            head = core * n + jb
            a00, a01 = decay(0, head), decay(1, head)
            a10, a11 = decay(2, head), decay(3, head)
            x_copy(1, jb).wait_recv()

            @pl.when(has_up)
            def _():
                z_copy(1, jb).wait_recv()

            after = zrx[1, jb]
            middle = (a10 * a11) * after + chips[1, 1, jb]

            @pl.when(has_down)
            def _():
                ztx[1, jb] = (a00 * a01) * middle + chips[0, 1, jb]
                z_copy(1, jb).start()

            into = jnp.where(x == 1, after, middle)
            res[1, 1, jb] = into
            res[0, 1, jb] = decay(2 * x + 1, head) * into + pair[1, jb, 1]
            s_copy(1, jb).start()

        jo = t - lag

        @pl.when(jnp.logical_and(jo >= 0, jo < n))
        def _():
            outputs(core * n + jo, res[core, 0, jo], res[core, 1, jo])
            s_copy(0, jo).wait_recv()
            s_copy(1, jo).wait_recv()
            outputs((1 - core) * n + jo, srx[0, jo], srx[1, jo])

        return carry

    lax.fori_loop(0, n + planes, second, 0)

    for copy in dec_copies:
        copy.wait_send()

    def drain(j, carry):
        pair_copy(j).wait_send()
        for d in (0, 1):
            x_copy(d, j).wait_send()
            s_copy(d, j).wait_send()

        @pl.when(has_up)
        def _():
            z_copy(0, j).wait_send()

        @pl.when(has_down)
        def _():
            z_copy(1, j).wait_send()

        return carry

    lax.fori_loop(0, n, drain, 0)


def on_device(planes, query_rows, key_rows, value_rows, log_decay, out_grad):
    heads = log_decay.shape[0]
    width = query_rows.shape[1] // heads
    n = heads // 2
    cumulative = jnp.cumsum(log_decay, axis=1)
    carried = jnp.broadcast_to(jnp.exp(cumulative[:, -1:]), (heads, width))
    square = (width, width)
    dma = pltpu.SemaphoreType.DMA
    shape = jax.ShapeDtypeStruct(query_rows.shape, BF16)
    return pl.pallas_call(
        functools.partial(kernel, planes),
        out_shape=(shape,) * 4,
        in_specs=[pl.BlockSpec(memory_space=pltpu.VMEM)] * 6,
        out_specs=(pl.BlockSpec(memory_space=pltpu.VMEM),) * 4,
        scratch_shapes=[
            pltpu.VMEM((2, n, 2) + square, F32),
            pltpu.VMEM((n, 2) + square, F32),
            pltpu.VMEM((2, 2, n) + square, F32),
            pltpu.VMEM((2, n) + square, F32),
            pltpu.VMEM((2, n) + square, F32),
            pltpu.VMEM((2, 2, n) + square, F32),
            pltpu.VMEM((2, n) + square, F32),
            pltpu.VMEM((4, heads, width), F32),
            dma((3,)),
            dma((3,)),
            dma((n,)),
            dma((n,)),
            dma((2, n)),
            dma((2, n)),
            dma((2, n)),
            dma((2, n)),
            dma((2, n)),
            dma((2, n)),
        ],
        compiler_params=pltpu.CompilerParams(
            collective_id=0, has_side_effects=True, vmem_limit_bytes=48 * 1024 * 1024
        ),
    )(query_rows, key_rows, value_rows, out_grad, cumulative, carried)


def solution(mesh):
    rows = P(("grp", "seq"), None)
    in_specs = (rows, rows, rows, P(None, ("grp", "seq")), rows)
    return jax.shard_map(
        functools.partial(on_device, mesh.shape["seq"] // 4),
        mesh=mesh,
        in_specs=in_specs,
        out_specs=(rows,) * 4,
        check_vma=False,
    )
```

time: 418 us -> 91.4 us (0.22)
  waiting for transfers between devices: 336 us -> 0 us
  Pallas kernels: 0 us -> 83.3 us
  other arithmetic: 31.3 us -> 0.68 us
  matrix products: 29.8 us -> 0 us
  starting transfers between devices: 12.5 us -> 0 us
    ppermute x11 -> x0, waiting for transfers between devices: 336 us -> none  [partner_2(): return lax.ppermute(value, axis, pairs)]
    pallas_call x0 -> x1, Pallas kernels: none -> 83.3 us  [on_device(): pl.pallas_call(functools.partial(kernel, planes), out_shape=(shape,) * 4,...]
    dot_general x12 -> x0, matrix products: 29.8 us -> none  [the longest x1 4.96 us: on_device(): jnp.einsum('thd,the->hde', weighted_keys, values, preferred_element_type=...]
    select_n x4 -> x0, other arithmetic: 21.1 us -> none  [choose_tree(): jnp.where(flag, first_leaf, second_leaf)]
    ppermute x11 -> x0, starting transfers between devices: 12.5 us -> none  [partner_2(): return lax.ppermute(value, axis, pairs)]
    convert_element_type x2 -> x0, other arithmetic: 9.4 us -> none  [the longest x1 4.87 us: on_device(): state_in_rounded = state_in.astype(jnp.bfloat16)]
    reshape x3 -> x1, local copies, waits for them, and re-layouts: 5.19 us -> 0.76 us  [the longest x2 4.3 us: join_rows(): return array.astype(jnp.bfloat16).reshape(length, heads * width)]
  transfers between devices with their start and end apart: 11 -> 0, of which waited for: 6 -> 0; matrix products, arithmetic and copies ran while one was open for 7% -> 0% of each run, Pallas kernels for 0% -> 0%
where the time goes in v1:
time: 91.4 us; the launch traced here: 91.2 us
  Pallas kernels  83.3 us (91%)
  local copies, waits for them, and re-layouts  6.6 us (7%)
    pallas_call x1, Pallas kernels, on_device(): pl.pallas_call(functools.partial(kernel, planes), out_shape=(shape,) * 4,...  83.3 us
    unnamed x6, local copies, waits for them, and re-layouts  5.4 us

profile of v1, /device:TPU:0, one launch (start us, length us, event | category | flops | bytes accessed | tf_op | source)
XLA Modules:
  0.0 91.2 jit_solution(3178788833287806354)
XLA Ops:
  0.6 0.8 copy_bitcast_fusion.1
  1.4 0.6 reduce-window.6
  2.0 0.2 slice_reduce_fusion
  2.2 0.1 copy_bitcast_fusion
  2.2 0.2 fusion
  2.4 0.1 broadcast_in_dim.8.a_ref
  2.5 83.3 %shard_map.84 = (bf16[192,4096]{1,0:T(8,128)(2,1)S(1)}, bf16[192,4096]{1,0:T(8,128)(2,1)S(1)}, bf16[192,4096]{1,0:T(8,128)(2,1)S(1)}, bf16[192,4096]{1,0:T(8,128)(2,1)}) custom-call(bf16[192,4096]{1,0:T(8,128)(2,1)} %q_ref.1, bf16[192,4096]{1,0:T(8,128)(2,1)} %k_ref.1, bf16[192,4096]{1,0:T(8,128)(2,1)} %v_ref.1, bf16[192,4096]{1,0:T(8,128)(2,1)} %g_ref.1, ...), custom_call_target="tpu_custom_call" | custom-call | tf_op jit(solution)/shard_map/pallas_call | solution.py:283
  85.8 1.1 %copy.21 = bf16[192,4096]{1,0:T(8,128)(2,1)} copy(bf16[192,4096]{1,0:T(8,128)(2,1)S(1)} %get-tuple-element.8) | data formatting | bytes 3145728
  86.9 1.1 %copy.22 = bf16[192,4096]{1,0:T(8,128)(2,1)} copy(bf16[192,4096]{1,0:T(8,128)(2,1)S(1)} %get-tuple-element.9) | data formatting | bytes 3145728
  88.1 0.0 copy-start
  88.1 1.1 %copy.23 = bf16[192,4096]{1,0:T(8,128)(2,1)} copy(bf16[192,4096]{1,0:T(8,128)(2,1)S(1)} %get-tuple-element.10) | data formatting | bytes 3145728
  89.2 0.8 copy-done
  90.0 1.1 %copy.24 = bf16[192,4096]{1,0:T(8,128)(2,1)} copy(bf16[192,4096]{1,0:T(8,128)(2,1)S(1)} %copy-done) | data formatting | bytes 3145728
  (2 shorter events, 0.0 us)
Async XLA Ops:
  88.1 2.0 %copy-start = (bf16[192,4096]{1,0:T(8,128)(2,1)S(1)}, bf16[192,4096]{1,0:T(8,128)(2,1)}, u32[]{:S(2)}) copy-start(bf16[192,4096]{1,0:T(8,128)(2,1)} %get-tuple-element.11) | copy-start | bytes 4718596

commit v2 on v1

--- a/solution.py
+++ b/solution.py
@@ -9,6 +9,7 @@
 
 F32 = jnp.float32
 BF16 = jnp.bfloat16
+HOP_SLOTS = 2
 
 
 def dot(a, b, a_dim, b_dim):
@@ -17,16 +18,18 @@
 
 def kernel(
     planes,
-    q_ref,
-    k_ref,
-    v_ref,
-    g_ref,
+    q_in,
+    k_in,
+    v_in,
+    g_in,
+    log_ref,
+    att_out,
+    qg_out,
+    kg_out,
+    vg_out,
+    rows,
+    outs,
     cum_ref,
-    a_ref,
-    att_ref,
-    qg_ref,
-    kg_ref,
-    vg_ref,
     pair,
     give,
     chips,
@@ -35,6 +38,8 @@
     res,
     srx,
     dec,
+    in_sem,
+    out_sem,
     dec_send,
     dec_recv,
     pair_send,
@@ -48,7 +53,8 @@
 ):
     n = pair.shape[1]
     width = pair.shape[-1]
-    length = q_ref.shape[0]
+    length = rows.shape[1]
+    q_ref, k_ref, v_ref, g_ref = (rows.at[i] for i in range(4))
     seq = lax.axis_index("seq")
     core = lax.rem(seq, 2)
     x = lax.rem(seq // 2, 2)
@@ -61,6 +67,13 @@
     has_down = z > 0
     has_up = z < planes - 1
 
+    loads = [
+        pltpu.make_async_copy(src, rows.at[i], in_sem.at[i])
+        for i, src in enumerate((q_in, k_in, v_in, g_in))
+    ]
+    for load in loads:
+        load.start()
+
     barrier = pltpu.get_barrier_semaphore()
     for peer in (sibling, across, diagonal):
         pl.semaphore_signal(barrier, inc=1, device_id={"seq": peer})
@@ -72,6 +85,17 @@
     @pl.when(has_up)
     def _():
         pl.semaphore_signal(barrier, inc=1, device_id={"seq": seq + 4})
+
+    row_index = lax.broadcasted_iota(jnp.int32, (length, length), 0)
+    col_index = lax.broadcasted_iota(jnp.int32, (length, length), 1)
+    cum_ref[...] = lax.dot_general(
+        log_ref[...],
+        (row_index <= col_index).astype(F32),
+        (((1,), (0,)), ((), ())),
+        precision=lax.Precision.HIGHEST,
+        preferred_element_type=F32,
+    )
+    dec[place] = jnp.broadcast_to(jnp.exp(cum_ref[:, length - 1 : length]), dec.shape[1:])
 
     pl.semaphore_wait(barrier, 3 + has_down.astype(jnp.int32) + has_up.astype(jnp.int32))
 
@@ -81,7 +105,7 @@
         )
 
     def dec_copy(slot, peer):
-        return remote(a_ref, dec.at[place], dec_send.at[slot], dec_recv.at[slot], peer)
+        return remote(dec.at[place], dec.at[place], dec_send.at[slot], dec_recv.at[slot], peer)
 
     def pair_copy(j):
         return remote(give.at[j], pair.at[core, j], pair_send.at[j], pair_recv.at[j], sibling)
@@ -103,10 +127,8 @@
     dec_copies = [dec_copy(0, sibling), dec_copy(1, across), dec_copy(2, diagonal)]
     for copy in dec_copies:
         copy.start()
-    dec[place] = a_ref[...]
-
-    row_index = lax.broadcasted_iota(jnp.int32, (length, length), 0)
-    col_index = lax.broadcasted_iota(jnp.int32, (length, length), 1)
+    for load in loads:
+        load.wait()
 
     def column(row):
         return jnp.sum(jnp.where(row_index == col_index, row, 0.0), axis=1, keepdims=True)
@@ -161,6 +183,8 @@
     @pl.when(jnp.logical_not(has_up))
     def _():
         zrx[1] = jnp.zeros(zrx.shape[1:], F32)
+
+    results = (att_out, qg_out, kg_out, vg_out)
 
     def outputs(head, state, grad):
         cols = lanes(head)
@@ -176,15 +200,17 @@
         to_end = jnp.exp(total - col)
         state = state.astype(BF16)
         grad = grad.astype(BF16)
-        att_ref[:, cols] = (dot(weights, v, 1, 0) + to_query * dot(q, state, 1, 0)).astype(BF16)
-        qg_ref[:, cols] = (dot(scores, k, 1, 0) + to_query * dot(g, state, 1, 1)).astype(BF16)
-        kg_ref[:, cols] = (dot(scores, q, 0, 0) + to_end * dot(v, grad, 1, 1)).astype(BF16)
-        vg_ref[:, cols] = (dot(weights, g, 0, 0) + to_end * dot(k, grad, 1, 0)).astype(BF16)
-
-    lag = jnp.maximum(z, planes - 1 - z) + 1
+        outs[0, :, cols] = (dot(weights, v, 1, 0) + to_query * dot(q, state, 1, 0)).astype(BF16)
+        outs[1, :, cols] = (dot(scores, k, 1, 0) + to_query * dot(g, state, 1, 1)).astype(BF16)
+        outs[2, :, cols] = (dot(scores, q, 0, 0) + to_end * dot(v, grad, 1, 1)).astype(BF16)
+        outs[3, :, cols] = (dot(weights, g, 0, 0) + to_end * dot(k, grad, 1, 0)).astype(BF16)
+        for i, dst in enumerate(results):
+            pltpu.make_async_copy(outs.at[i, :, cols], dst.at[:, cols], out_sem.at[i]).start()
+
+    lag = HOP_SLOTS * jnp.maximum(z, planes - 1 - z) + 1
 
     def second(t, carry):
-        jf = t - z
+        jf = t - HOP_SLOTS * z
 
         @pl.when(jnp.logical_and(jf >= 0, jf < n))
         def _():
@@ -210,7 +236,7 @@
             res[1, 0, jf] = decay(2 * x, head) * into + pair[0, jf, 0]
             s_copy(0, jf).start()
 
-        jb = t - (planes - 1 - z)
+        jb = t - HOP_SLOTS * (planes - 1 - z)
 
         @pl.when(jnp.logical_and(jb >= 0, jb < n))
         def _():
@@ -247,8 +273,10 @@
 
         return carry
 
-    lax.fori_loop(0, n + planes, second, 0)
-
+    lax.fori_loop(0, n + HOP_SLOTS * (planes - 1) + 1, second, 0)
+
+    for i, dst in enumerate(results):
+        pltpu.make_async_copy(outs.at[i], dst, out_sem.at[i]).wait()
     for copy in dec_copies:
         copy.wait_send()
 
@@ -275,17 +303,19 @@
     heads = log_decay.shape[0]
     width = query_rows.shape[1] // heads
     n = heads // 2
-    cumulative = jnp.cumsum(log_decay, axis=1)
-    carried = jnp.broadcast_to(jnp.exp(cumulative[:, -1:]), (heads, width))
     square = (width, width)
     dma = pltpu.SemaphoreType.DMA
     shape = jax.ShapeDtypeStruct(query_rows.shape, BF16)
     return pl.pallas_call(
         functools.partial(kernel, planes),
         out_shape=(shape,) * 4,
-        in_specs=[pl.BlockSpec(memory_space=pltpu.VMEM)] * 6,
-        out_specs=(pl.BlockSpec(memory_space=pltpu.VMEM),) * 4,
+        in_specs=[pl.BlockSpec(memory_space=pl.ANY)] * 4
+        + [pl.BlockSpec(memory_space=pltpu.VMEM)],
+        out_specs=(pl.BlockSpec(memory_space=pl.ANY),) * 4,
         scratch_shapes=[
+            pltpu.VMEM((4,) + query_rows.shape, BF16),
+            pltpu.VMEM((4,) + query_rows.shape, BF16),
+            pltpu.VMEM(log_decay.shape, F32),
             pltpu.VMEM((2, n, 2) + square, F32),
             pltpu.VMEM((n, 2) + square, F32),
             pltpu.VMEM((2, 2, n) + square, F32),
@@ -294,6 +324,8 @@
             pltpu.VMEM((2, 2, n) + square, F32),
             pltpu.VMEM((2, n) + square, F32),
             pltpu.VMEM((4, heads, width), F32),
+            dma((4,)),
+            dma((4,)),
             dma((3,)),
             dma((3,)),
             dma((n,)),
@@ -308,7 +340,7 @@
         compiler_params=pltpu.CompilerParams(
             collective_id=0, has_side_effects=True, vmem_limit_bytes=48 * 1024 * 1024
         ),
-    )(query_rows, key_rows, value_rows, out_grad, cumulative, carried)
+    )(query_rows, key_rows, value_rows, out_grad, log_decay)
 
 
 def solution(mesh):

time: 91.4 us -> 77.1 us (0.84)
  Pallas kernels: 83.3 us -> 70.1 us
    pallas_call x1, Pallas kernels: 83.3 us -> 70.1 us  [on_device(): pl.pallas_call(functools.partial(kernel, planes), out_shape=(shape,) * 4,...]
    unnamed x6 -> x8, local copies, waits for them, and re-layouts: 5.4 us -> 6.16 us
where the time goes in v2:
time: 77.1 us; the launch traced here: 76.9 us
  Pallas kernels  70.1 us (91%)
  local copies, waits for them, and re-layouts  6.16 us (8%)
    pallas_call x1, Pallas kernels, on_device(): pl.pallas_call(functools.partial(kernel, planes), out_shape=(shape,) * 4,...  70.1 us
    unnamed x8, local copies, waits for them, and re-layouts  6.16 us

profile of v2, /device:TPU:0, one launch (start us, length us, event | category | flops | bytes accessed | tf_op | source)
XLA Modules:
  0.0 76.9 jit_solution(1441633904864240957)
XLA Ops:
  0.6 0.0 copy-start
  0.6 0.7 copy-done
  1.4 70.1 %shard_map.84 = (bf16[192,4096]{1,0:T(8,128)(2,1)S(1)}, bf16[192,4096]{1,0:T(8,128)(2,1)S(1)}, bf16[192,4096]{1,0:T(8,128)(2,1)S(1)}, bf16[192,4096]{1,0:T(8,128)(2,1)}) custom-call(bf16[192,4096]{1,0:T(8,128)(2,1)} %q_in.1, bf16[192,4096]{1,0:T(8,128)(2,1)} %k_in.1, bf16[192,4096]{1,0:T(8,128)(2,1)} %v_in.1, bf16[192,4096]{1,0:T(8,128)(2,1)} %g_in.1, ...), custom_call_target="tpu_custom_call" | custom-call | tf_op jit(solution)/shard_map/pallas_call | solution.py:309
  71.5 1.1 %copy.13 = bf16[192,4096]{1,0:T(8,128)(2,1)} copy(bf16[192,4096]{1,0:T(8,128)(2,1)S(1)} %get-tuple-element.8) | data formatting | bytes 3145728
  72.6 1.1 %copy.14 = bf16[192,4096]{1,0:T(8,128)(2,1)} copy(bf16[192,4096]{1,0:T(8,128)(2,1)S(1)} %get-tuple-element.9) | data formatting | bytes 3145728
  73.8 0.0 copy-start.1
  73.8 1.1 %copy.15 = bf16[192,4096]{1,0:T(8,128)(2,1)} copy(bf16[192,4096]{1,0:T(8,128)(2,1)S(1)} %get-tuple-element.10) | data formatting | bytes 3145728
  74.9 0.8 %copy-done.1 = bf16[192,4096]{1,0:T(8,128)(2,1)S(1)} copy-done((bf16[192,4096]{1,0:T(8,128)(2,1)S(1)}, bf16[192,4096]{1,0:T(8,128)(2,1)}, u32[]{:S(2)}) %copy-start.1) | copy-done | bytes 1572888
  75.7 1.1 %copy.16 = bf16[192,4096]{1,0:T(8,128)(2,1)} copy(bf16[192,4096]{1,0:T(8,128)(2,1)S(1)} %copy-done.1) | data formatting | bytes 3145728
Async XLA Ops:
  0.6 0.8 copy-start
  73.8 2.0 %copy-start.1 = (bf16[192,4096]{1,0:T(8,128)(2,1)S(1)}, bf16[192,4096]{1,0:T(8,128)(2,1)}, u32[]{:S(2)}) copy-start(bf16[192,4096]{1,0:T(8,128)(2,1)} %get-tuple-element.11) | copy-start | bytes 4718596

commit v3 on v2

--- a/solution.py
+++ b/solution.py
@@ -9,7 +9,7 @@
 
 F32 = jnp.float32
 BF16 = jnp.bfloat16
-HOP_SLOTS = 2
+HOP_SLOTS = 3
 
 
 def dot(a, b, a_dim, b_dim):
@@ -149,6 +149,9 @@
         dst[0] = dot(weighted, v_ref[:, cols], 0, 0)
         dst[1] = dot(scaled, g_ref[:, cols], 0, 0)
 
+    lead = jnp.where(2 * z <= planes - 1, 0, 1)
+    offset = HOP_SLOTS * jnp.abs(planes - 1 - 2 * z)
+
     def first(i, carry):
         @pl.when(i < n)
         def _():
@@ -166,13 +169,25 @@
             head = core * n + j
             pair_copy(j).wait_recv()
             chips[x, 0, j] = decay(2 * x + 1, head) * pair[0, j, 0] + pair[1, j, 0]
-            x_copy(0, j).start()
             chips[x, 1, j] = decay(2 * x, head) * pair[1, j, 1] + pair[0, j, 1]
-            x_copy(1, j).start()
+            x_copy(lead, j).start()
+
+            @pl.when(j >= offset)
+            def _():
+                x_copy(1 - lead, j - offset).start()
 
         return carry
 
     lax.fori_loop(0, n + 1, first, 0)
+
+    def rest(j, carry):
+        @pl.when(j + offset >= n)
+        def _():
+            x_copy(1 - lead, j).start()
+
+        return carry
+
+    lax.fori_loop(0, n, rest, 0)
     dec_copies[1].wait_recv()
     dec_copies[2].wait_recv()
 

time: 77.1 us -> 70.3 us (0.912)
  Pallas kernels: 70.1 us -> 63.2 us
    pallas_call x1, Pallas kernels: 70.1 us -> 63.2 us  [on_device(): pl.pallas_call(functools.partial(kernel, planes), out_shape=(shape,) * 4,...]
where the time goes in v3:
time: 70.3 us; the launch traced here: 70 us
  Pallas kernels  63.2 us (90%)
  local copies, waits for them, and re-layouts  6.16 us (9%)
    pallas_call x1, Pallas kernels, on_device(): pl.pallas_call(functools.partial(kernel, planes), out_shape=(shape,) * 4,...  63.2 us
    unnamed x8, local copies, waits for them, and re-layouts  6.16 us

profile of v3, /device:TPU:0, one launch (start us, length us, event | category | flops | bytes accessed | tf_op | source)
XLA Modules:
  0.0 70.0 jit_solution(16022058143432974280)
XLA Ops:
  0.6 0.0 copy-start
  0.6 0.7 %copy-done = f32[32,192]{1,0:T(8,128)S(1)} copy-done((f32[32,192]{1,0:T(8,128)S(1)}, f32[32,192]{1,0:T(8,128)}, u32[]{:S(2)}) %copy-start) | copy-done | bytes 24600
  1.4 63.2 %shard_map.84 = (bf16[192,4096]{1,0:T(8,128)(2,1)S(1)}, bf16[192,4096]{1,0:T(8,128)(2,1)S(1)}, bf16[192,4096]{1,0:T(8,128)(2,1)S(1)}, bf16[192,4096]{1,0:T(8,128)(2,1)}) custom-call(bf16[192,4096]{1,0:T(8,128)(2,1)} %q_in.1, bf16[192,4096]{1,0:T(8,128)(2,1)} %k_in.1, bf16[192,4096]{1,0:T(8,128)(2,1)} %v_in.1, bf16[192,4096]{1,0:T(8,128)(2,1)} %g_in.1, ...), custom_call_target="tpu_custom_call" | custom-call | tf_op jit(solution)/shard_map/pallas_call | solution.py:324
  64.6 1.1 %copy.13 = bf16[192,4096]{1,0:T(8,128)(2,1)} copy(bf16[192,4096]{1,0:T(8,128)(2,1)S(1)} %get-tuple-element.8) | data formatting | bytes 3145728
  65.8 1.1 %copy.14 = bf16[192,4096]{1,0:T(8,128)(2,1)} copy(bf16[192,4096]{1,0:T(8,128)(2,1)S(1)} %get-tuple-element.9) | data formatting | bytes 3145728
  66.9 0.0 copy-start.1
  66.9 1.1 %copy.15 = bf16[192,4096]{1,0:T(8,128)(2,1)} copy(bf16[192,4096]{1,0:T(8,128)(2,1)S(1)} %get-tuple-element.10) | data formatting | bytes 3145728
  68.1 0.8 %copy-done.1 = bf16[192,4096]{1,0:T(8,128)(2,1)S(1)} copy-done((bf16[192,4096]{1,0:T(8,128)(2,1)S(1)}, bf16[192,4096]{1,0:T(8,128)(2,1)}, u32[]{:S(2)}) %copy-start.1) | copy-done | bytes 1572888
  68.9 1.1 %copy.16 = bf16[192,4096]{1,0:T(8,128)(2,1)} copy(bf16[192,4096]{1,0:T(8,128)(2,1)S(1)} %copy-done.1) | data formatting | bytes 3145728
Async XLA Ops:
  0.6 0.8 %copy-start = (f32[32,192]{1,0:T(8,128)S(1)}, f32[32,192]{1,0:T(8,128)}, u32[]{:S(2)}) copy-start(f32[32,192]{1,0:T(8,128)} %log_ref.1) | copy-start | bytes 73732
  66.9 2.0 %copy-start.1 = (bf16[192,4096]{1,0:T(8,128)(2,1)S(1)}, bf16[192,4096]{1,0:T(8,128)(2,1)}, u32[]{:S(2)}) copy-start(bf16[192,4096]{1,0:T(8,128)(2,1)} %get-tuple-element.11) | copy-start | bytes 4718596

commit v4 on v3

--- a/solution.py
+++ b/solution.py
@@ -157,7 +157,6 @@
         def _():
             local_states((1 - core) * n + i, give.at[i])
             pair_copy(i).start()
-            local_states(core * n + i, pair.at[core, i])
 
         @pl.when(i == 1)
         def _():
@@ -175,6 +174,10 @@
             @pl.when(j >= offset)
             def _():
                 x_copy(1 - lead, j - offset).start()
+
+        @pl.when(i < n)
+        def _():
+            local_states(core * n + i, pair.at[core, i])
 
         return carry
 

time: 70.3 us -> 69.7 us (level)
  no operation moved by 1% of the time
where the time goes in v4:
time: 69.7 us; the launch traced here: 69.5 us
  Pallas kernels  62.7 us (90%)
  local copies, waits for them, and re-layouts  6.16 us (9%)
    pallas_call x1, Pallas kernels, on_device(): pl.pallas_call(functools.partial(kernel, planes), out_shape=(shape,) * 4,...  62.7 us
    unnamed x8, local copies, waits for them, and re-layouts  6.16 us

profile of v4, /device:TPU:0, one launch (start us, length us, event | category | flops | bytes accessed | tf_op | source)
XLA Modules:
  0.0 69.5 jit_solution(2136354573950947004)
XLA Ops:
  0.6 0.0 copy-start
  0.6 0.7 %copy-done = f32[32,192]{1,0:T(8,128)S(1)} copy-done((f32[32,192]{1,0:T(8,128)S(1)}, f32[32,192]{1,0:T(8,128)}, u32[]{:S(2)}) %copy-start) | copy-done | bytes 24600
  1.4 62.7 %shard_map.84 = (bf16[192,4096]{1,0:T(8,128)(2,1)S(1)}, bf16[192,4096]{1,0:T(8,128)(2,1)S(1)}, bf16[192,4096]{1,0:T(8,128)(2,1)S(1)}, bf16[192,4096]{1,0:T(8,128)(2,1)}) custom-call(bf16[192,4096]{1,0:T(8,128)(2,1)} %q_in.1, bf16[192,4096]{1,0:T(8,128)(2,1)} %k_in.1, bf16[192,4096]{1,0:T(8,128)(2,1)} %v_in.1, bf16[192,4096]{1,0:T(8,128)(2,1)} %g_in.1, ...), custom_call_target="tpu_custom_call" | custom-call | tf_op jit(solution)/shard_map/pallas_call | solution.py:327
  64.1 1.1 %copy.13 = bf16[192,4096]{1,0:T(8,128)(2,1)} copy(bf16[192,4096]{1,0:T(8,128)(2,1)S(1)} %get-tuple-element.8) | data formatting | bytes 3145728
  65.3 1.1 %copy.14 = bf16[192,4096]{1,0:T(8,128)(2,1)} copy(bf16[192,4096]{1,0:T(8,128)(2,1)S(1)} %get-tuple-element.9) | data formatting | bytes 3145728
  66.4 0.0 copy-start.1
  66.4 1.1 %copy.15 = bf16[192,4096]{1,0:T(8,128)(2,1)} copy(bf16[192,4096]{1,0:T(8,128)(2,1)S(1)} %get-tuple-element.10) | data formatting | bytes 3145728
  67.5 0.8 %copy-done.1 = bf16[192,4096]{1,0:T(8,128)(2,1)S(1)} copy-done((bf16[192,4096]{1,0:T(8,128)(2,1)S(1)}, bf16[192,4096]{1,0:T(8,128)(2,1)}, u32[]{:S(2)}) %copy-start.1) | copy-done | bytes 1572888
  68.4 1.1 %copy.16 = bf16[192,4096]{1,0:T(8,128)(2,1)} copy(bf16[192,4096]{1,0:T(8,128)(2,1)S(1)} %copy-done.1) | data formatting | bytes 3145728
Async XLA Ops:
  0.6 0.8 %copy-start = (f32[32,192]{1,0:T(8,128)S(1)}, f32[32,192]{1,0:T(8,128)}, u32[]{:S(2)}) copy-start(f32[32,192]{1,0:T(8,128)} %log_ref.1) | copy-start | bytes 73732
  66.4 2.0 %copy-start.1 = (bf16[192,4096]{1,0:T(8,128)(2,1)S(1)}, bf16[192,4096]{1,0:T(8,128)(2,1)}, u32[]{:S(2)}) copy-start(bf16[192,4096]{1,0:T(8,128)(2,1)} %get-tuple-element.11) | copy-start | bytes 4718596

commit v5 on v4

--- a/solution.py
+++ b/solution.py
@@ -9,7 +9,7 @@
 
 F32 = jnp.float32
 BF16 = jnp.bfloat16
-HOP_SLOTS = 3
+HOP_SLOTS = 5
 
 
 def dot(a, b, a_dim, b_dim):

time: 69.7 us -> 69.7 us (level)
  no operation moved by 1% of the time
where the time goes in v5:
time: 69.7 us; the launch traced here: 69.5 us
  Pallas kernels  62.7 us (90%)
  local copies, waits for them, and re-layouts  6.16 us (9%)
    pallas_call x1, Pallas kernels, on_device(): pl.pallas_call(functools.partial(kernel, planes), out_shape=(shape,) * 4,...  62.7 us
    unnamed x8, local copies, waits for them, and re-layouts  6.16 us

profile of v5, /device:TPU:0, one launch (start us, length us, event | category | flops | bytes accessed | tf_op | source)
XLA Modules:
  0.0 69.5 jit_solution(4358755118835617583)
XLA Ops:
  0.6 0.0 copy-start
  0.6 0.7 %copy-done = f32[32,192]{1,0:T(8,128)S(1)} copy-done((f32[32,192]{1,0:T(8,128)S(1)}, f32[32,192]{1,0:T(8,128)}, u32[]{:S(2)}) %copy-start) | copy-done | bytes 24600
  1.4 62.7 %shard_map.84 = (bf16[192,4096]{1,0:T(8,128)(2,1)S(1)}, bf16[192,4096]{1,0:T(8,128)(2,1)S(1)}, bf16[192,4096]{1,0:T(8,128)(2,1)S(1)}, bf16[192,4096]{1,0:T(8,128)(2,1)}) custom-call(bf16[192,4096]{1,0:T(8,128)(2,1)} %q_in.1, bf16[192,4096]{1,0:T(8,128)(2,1)} %k_in.1, bf16[192,4096]{1,0:T(8,128)(2,1)} %v_in.1, bf16[192,4096]{1,0:T(8,128)(2,1)} %g_in.1, ...), custom_call_target="tpu_custom_call" | custom-call | tf_op jit(solution)/shard_map/pallas_call | solution.py:327
  64.1 1.1 %copy.13 = bf16[192,4096]{1,0:T(8,128)(2,1)} copy(bf16[192,4096]{1,0:T(8,128)(2,1)S(1)} %get-tuple-element.8) | data formatting | bytes 3145728
  65.3 1.1 %copy.14 = bf16[192,4096]{1,0:T(8,128)(2,1)} copy(bf16[192,4096]{1,0:T(8,128)(2,1)S(1)} %get-tuple-element.9) | data formatting | bytes 3145728
  66.4 0.0 copy-start.1
  66.4 1.1 %copy.15 = bf16[192,4096]{1,0:T(8,128)(2,1)} copy(bf16[192,4096]{1,0:T(8,128)(2,1)S(1)} %get-tuple-element.10) | data formatting | bytes 3145728
  67.5 0.8 %copy-done.1 = bf16[192,4096]{1,0:T(8,128)(2,1)S(1)} copy-done((bf16[192,4096]{1,0:T(8,128)(2,1)S(1)}, bf16[192,4096]{1,0:T(8,128)(2,1)}, u32[]{:S(2)}) %copy-start.1) | copy-done | bytes 1572888
  68.4 1.1 %copy.16 = bf16[192,4096]{1,0:T(8,128)(2,1)} copy(bf16[192,4096]{1,0:T(8,128)(2,1)S(1)} %copy-done.1) | data formatting | bytes 3145728
Async XLA Ops:
  0.6 0.8 %copy-start = (f32[32,192]{1,0:T(8,128)S(1)}, f32[32,192]{1,0:T(8,128)}, u32[]{:S(2)}) copy-start(f32[32,192]{1,0:T(8,128)} %log_ref.1) | copy-start | bytes 73732
  66.4 2.0 %copy-start.1 = (bf16[192,4096]{1,0:T(8,128)(2,1)S(1)}, bf16[192,4096]{1,0:T(8,128)(2,1)}, u32[]{:S(2)}) copy-start(bf16[192,4096]{1,0:T(8,128)(2,1)} %get-tuple-element.11) | copy-start | bytes 4718596
